TPU v7x, 256 devices: a whole 4x4x8 slice. The times are simulated.
256 devices in a mesh: freq: 4 (over x_hi, core), xband: 64 (over y, z, x_lo).
Axes of the slice: x: 4 (x_hi: 2, x_lo: 2; x = x_hi * 2 + x_lo), y: 4, z: 8, core: 2. Of those that a mesh axis runs over, the one named last changes fastest.
Arguments:
- source_field: float32 [8, 2, 1024, 2048], P('freq', None, 'xband'), may hold values from -6 to 6
- receiver_field: float32 [8, 2, 1024, 2048], P('freq', None, 'xband'), may hold values from -6 to 6
- adjoint_field: float32 [8, 2, 1024, 2048], P('freq', None, 'xband'), may hold values from -6 to 6
- slowness: float32 [4, 1024, 2048], P('freq', 'xband'), may hold values from 0.8 to 1.25
- epsilon_field: float32 [4, 1024, 2048], P('freq', 'xband'), may hold values from 0 to 0.25
- delta_field: float32 [4, 1024, 2048], P('freq', 'xband'), may hold values from 0 to 0.25
- depth_slab: int32 [4], replicated, may hold values from 0 to 3, each once
- freq_index: int32 [8], P('freq'), may hold values from 0 to 7, each once
Outputs:
- adjoint_final: float32 [8, 2, 1024, 2048], P('freq', None, 'xband')
- image_stack: float32 [4, 1024, 2048], P(None, 'xband')
- model_gradient: float32 [4, 3, 1024, 2048], P('freq', None, 'xband')
Inputs may be any that keep to these rules, and one draw needn't show every extreme that they name: `depth_slab`: each of the 4 slabs is used by exactly one depth step. `freq_index`: each frequency number is held by exactly one slot.
All inputs are finite; a program needn't handle non-finite values.
Results may differ from a plain program's by a relative error of at most 0.0001.
Values sent between devices are 32-bit elements; how exact they have to be, the bound alone decides.
A program may use at most 64 MiB of HBM per device.

v0:
```python
import jax
import jax.numpy as jnp
from jax import lax
from jax.sharding import PartitionSpec as P

BASE_FREQ = 2.0
FREQ_STEP = 0.25
DISPERSE = 0.08
DIFFUSE = 0.05
FORCING = 0.5


def broadcast(array, axis, root):
    mine = lax.axis_index(axis) == root
    return lax.psum(jnp.where(mine, array, jnp.zeros_like(array)), axis)


def extended(cells, sides, width):
    for axis, dim in sides:
        count = lax.axis_size(axis)
        ends = count - 1
        head = lax.slice_in_dim(cells, 0, width, axis=dim)
        tail = lax.slice_in_dim(cells, cells.shape[dim] - width, cells.shape[dim], axis=dim)
        cells = jnp.concatenate(
            [
                lax.ppermute(tail, axis, [(i, (i + 1) % count) for i in range(ends)]),
                cells,
                lax.ppermute(head, axis, [((i + 1) % count, i) for i in range(ends)]),
            ],
            axis=dim,
        )
    return cells


def body(
    source_field,
    receiver_field,
    adjoint_field,
    slowness,
    epsilon_field,
    delta_field,
    depth_slab,
    freq_index,
):
    freq_groups = lax.axis_size("freq")
    freq_count = source_field.shape[0] * freq_groups
    slab_local = slowness.shape[0]
    depth_count = depth_slab.shape[0]
    my_group = lax.axis_index("freq")
    angular = (BASE_FREQ + FREQ_STEP * freq_index.astype(jnp.float32))[:, None, None]
    field_signs = jnp.array([1.0, -1.0, -1.0], jnp.float32)[:, None, None, None]
    fields = jnp.stack([source_field, receiver_field, adjoint_field])
    model_slow, model_eps, model_del = (slowness, epsilon_field, delta_field)
    gradient = jnp.zeros((slab_local, 3) + slowness.shape[1:], jnp.float32)
    images = []
    for depth_step in range(depth_count):
        slab_index = depth_slab[depth_step]
        owner_index = slab_index // slab_local
        slot_index = slab_index % slab_local
        own_slow = lax.dynamic_index_in_dim(model_slow, slot_index, 0, False)
        own_eps = lax.dynamic_index_in_dim(model_eps, slot_index, 0, False)
        own_del = lax.dynamic_index_in_dim(model_del, slot_index, 0, False)
        slow_part, eps_part, del_part = (
            broadcast(own_slow, "freq", owner_index),
            broadcast(own_eps, "freq", owner_index),
            broadcast(own_del, "freq", owner_index),
        )
        phase_angle = field_signs * angular * (slow_part * (1.0 + eps_part))
        cosine = jnp.cos(phase_angle)
        sine_val = jnp.sin(phase_angle)
        real_part = fields[:, :, 0] * cosine - fields[:, :, 1] * sine_val
        imag_part = fields[:, :, 0] * sine_val + fields[:, :, 1] * cosine
        rotated = jnp.stack([real_part, imag_part], axis=2)
        padded = extended(rotated, (("xband", 3),), 1)
        inline = jnp.pad(rotated, ((0, 0), (0, 0), (0, 0), (0, 0), (1, 1)))
        laplacian = (
            padded[:, :, :, 2:]
            + padded[:, :, :, :-2]
            + inline[..., 2:]
            + inline[..., :-2]
            - 4.0 * rotated
        )
        coupling = (
            field_signs * DISPERSE * (1.0 + 2.0 * del_part) * BASE_FREQ / (angular * slow_part)
        )
        new_real = real_part + DIFFUSE * laplacian[:, :, 0] - coupling * laplacian[:, :, 1]
        new_imag = imag_part + DIFFUSE * laplacian[:, :, 1] + coupling * laplacian[:, :, 0]
        moved = jnp.stack([new_real, new_imag], axis=2)
        source_now = moved[0]
        receiver_now = moved[1]
        partial_image = jnp.sum(
            source_now[:, 0] * receiver_now[:, 0] + source_now[:, 1] * receiver_now[:, 1], axis=0
        )
        image_depth = lax.psum(partial_image, "freq") / freq_count
        images.append(image_depth)
        adjoint_now = moved[2] + FORCING * image_depth * source_now
        fields = jnp.stack([source_now, receiver_now, adjoint_now])
        slow_term = jnp.sum(
            angular * (source_now[:, 0] * adjoint_now[:, 1] - source_now[:, 1] * adjoint_now[:, 0]),
            axis=0,
        )
        aniso_term = jnp.sum(
            angular
            * (receiver_now[:, 0] * adjoint_now[:, 1] - receiver_now[:, 1] * adjoint_now[:, 0]),
            axis=0,
        )
        delta_term = jnp.sum(
            BASE_FREQ
            / angular
            * (source_now[:, 0] * adjoint_now[:, 0] + source_now[:, 1] * adjoint_now[:, 1]),
            axis=0,
        )
        grad_terms = jnp.stack([slow_term, aniso_term, delta_term])
        summed = lax.psum(grad_terms, "freq") / freq_count
        updated = lax.dynamic_update_index_in_dim(gradient, summed, slot_index, 0)
        gradient = jnp.where(owner_index == my_group, updated, gradient)
    return (fields[2], jnp.stack(images), gradient)


def solution(mesh):
    return jax.shard_map(
        body,
        mesh=mesh,
        in_specs=(
            P("freq", None, "xband", None),
            P("freq", None, "xband", None),
            P("freq", None, "xband", None),
            P("freq", "xband", None),
            P("freq", "xband", None),
            P("freq", "xband", None),
            P(),
            P("freq"),
        ),
        out_specs=(
            P("freq", None, "xband", None),
            P(None, "xband", None),
            P("freq", None, "xband", None),
        ),
        check_vma=False,
    )
```

profile of v0, /device:TPU:1, one launch (start us, length us, event | category | flops | bytes accessed | tf_op | source)
XLA Modules:
  0.0 408.1 jit_solution(12557518196832057713)
XLA Ops:
  7.2 1.5 fusion.85
  11.2 1.8 select_bitcast_fusion.12
  13.0 1.9 select_bitcast_fusion.1
  15.9 50.2 %all-reduce.26.cloned.1.call-done = (f32[16,2048]{1,0:T(8,128)}, f32[16,2048]{1,0:T(8,128)}, f32[16,2048]{1,0:T(8,128)}) async-done(((f32[16,2048]{1,0:T(8,128)}, f32[16,2048]{1,0:T(8,128)}, f32[16,2048]{1,0:T(8,128)}), (f32[16,2048]{1,0:T(8,128)}, f32[16,2048]{1,0:T(8,128)}, f32[16,2048]{1,0:T(8,128)})) %all-reduce.26.cloned.1.call-update) | async-done | bytes 393232 | tf_op jit(solution)/shard_map/psum | solution.py:15
  66.1 1.0 broadcast_multiply_fusion.4
  67.1 1.0 add_multiply_fusion.3
  68.1 0.9 multiply_add_fusion.10
  69.0 3.1 fusion.41
  72.3 1.3 collective-permute-start
  73.6 4.0 collective-permute-start.1
  79.2 0.9 fusion.2
  80.6 0.8 copy-done
  82.3 52.1 %all-reduce.24.cloned.1.call-done = (f32[16,2048]{1,0:T(8,128)}, f32[16,2048]{1,0:T(8,128)}, f32[16,2048]{1,0:T(8,128)}, f32[16,2048]{1,0:T(8,128)}) async-done(((f32[16,2048]{1,0:T(8,128)}, f32[16,2048]{1,0:T(8,128)}, f32[16,2048]{1,0:T(8,128)}, f32[16,2048]{1,0:T(8,128)}), (f32[16,2048]{1,0:T(8,128)}, f32[16,2048]{1,0:T(8,128)}, f32[16,2048]{1,0:T(8,128)}, ...) | async-done | bytes 524304 | tf_op jit(solution)/shard_map/psum | solution.py:15
  134.4 1.0 broadcast_multiply_fusion.3
  135.4 1.0 add_multiply_fusion.2
  136.4 0.9 multiply_add_fusion.9
  138.2 3.1 fusion.39
  141.4 1.3 collective-permute-start.2
  142.7 4.0 collective-permute-start.3
  147.6 0.8 collective-permute-done.3
  148.3 0.9 fusion.5
  149.8 0.8 copy-done.4
  151.3 0.9 bitcast_add_fusion
  152.3 51.2 %all-reduce.22.cloned.1.call-done = (f32[16,2048]{1,0:T(8,128)}, f32[16,2048]{1,0:T(8,128)}, f32[16,2048]{1,0:T(8,128)}, f32[16,2048]{1,0:T(8,128)}) async-done(((f32[16,2048]{1,0:T(8,128)}, f32[16,2048]{1,0:T(8,128)}, f32[16,2048]{1,0:T(8,128)}, f32[16,2048]{1,0:T(8,128)}), (f32[16,2048]{1,0:T(8,128)}, f32[16,2048]{1,0:T(8,128)}, f32[16,2048]{1,0:T(8,128)}, ...) | async-done | bytes 524304 | tf_op jit(solution)/shard_map/psum | solution.py:15
  203.5 1.0 broadcast_multiply_fusion.2
  204.6 1.0 add_multiply_fusion.1
  205.5 0.9 multiply_add_fusion.8
  207.3 3.1 fusion.37
  210.5 1.3 collective-permute-start.4
  211.8 4.2 %collective-permute-start.5 = (f32[3,2,2,1,2048]{4,3,1,2,0:T(1,128)S(1)}, f32[3,2,2,1,2048]{4,3,1,2,0:T(1,128)S(1)}, u32[]{:S(2)}, u32[]{:S(2)}) collective-permute-start(f32[3,2,2,1,2048]{4,3,1,2,0:T(1,128)S(1)} %get-tuple-element.58), channel_id=1, source_target_pairs={{0,1},{1,2},{2,3},{3,4},{4,5},{5,6},{6,7},{7,8},{8,9},{9,10},{10,1... | collective-permute-start | bytes 294920 | tf_op jit(solution)/shard_map/ppermute | solution.py:26
  216.7 0.8 collective-permute-done.5
  217.5 0.9 fusion.8
  220.4 0.9 bitcast_add_fusion.1
  221.4 51.2 %all-reduce.20.cloned.1.call-done = (f32[16,2048]{1,0:T(8,128)}, f32[16,2048]{1,0:T(8,128)}, f32[16,2048]{1,0:T(8,128)}, f32[16,2048]{1,0:T(8,128)}) async-done(((f32[16,2048]{1,0:T(8,128)}, f32[16,2048]{1,0:T(8,128)}, f32[16,2048]{1,0:T(8,128)}, f32[16,2048]{1,0:T(8,128)}), (f32[16,2048]{1,0:T(8,128)}, f32[16,2048]{1,0:T(8,128)}, f32[16,2048]{1,0:T(8,128)}, ...) | async-done | bytes 524304 | tf_op jit(solution)/shard_map/psum | solution.py:15
  272.6 1.6 multiply_bitcast_fusion.1
  274.2 0.9 bitcast_add_fusion.2
  275.1 0.8 copy-done.16
  276.1 3.1 fusion.36
  280.1 1.4 collective-permute-start.6
  281.6 4.0 collective-permute-start.7
  287.2 0.9 fusion.11
  289.5 0.8 pad_maximum_fusion.32
  290.2 49.2 %all-reduce.16.cloned.1.call-done = f32[16,2048]{1,0:T(8,128)} async-done(((f32[16,2048]{1,0:T(8,128)}), f32[16,2048]{1,0:T(8,128)}) %all-reduce.16.cloned.1.call-update) | async-done | bytes 131088 | tf_op jit(solution)/shard_map/psum | solution.py:94
  339.5 0.9 multiply_bitcast_fusion
  341.3 0.8 pad_maximum_fusion.29
  345.4 0.8 pad_maximum_fusion.28
  346.2 52.8 %all-reduce.18.cloned.1.call-done = (f32[3,16,2048]{2,1,0:T(8,128)}, f32[3,16,2048]{2,1,0:T(8,128)}, f32[3,16,2048]{2,1,0:T(8,128)}, f32[3,16,2048]{2,1,0:T(8,128)}) async-done(((f32[3,16,2048]{2,1,0:T(8,128)}, f32[3,16,2048]{2,1,0:T(8,128)}, f32[3,16,2048]{2,1,0:T(8,128)}, f32[3,16,2048]{2,1,0:T(8,128)}), (f32[3,16,2048]{2,1,0:T(8,128)}, f32[3,16,2048]{2,1,0:T(8,128)}, f32[3,16,2048]{2,1,0:T(8,128)}, ...) | async-done | bytes 1572880 | tf_op jit(solution)/shard_map/psum | solution.py:114
  399.1 2.2 select_bitcast_fusion
  (119 shorter events, 16.5 us)
Async XLA Ops:
  7.2 7.9 %copy-start.29 = (s32[2]{0:T(128)S(1)}, s32[2]{0:T(128)}, u32[]{:S(2)}) copy-start(s32[2]{0:T(128)} %param.16) | copy-start | bytes 28
  7.2 7.9 %copy-start.17 = (f32[2,2,16,2048]{3,2,1,0:T(8,128)S(1)}, f32[2,2,16,2048]{3,2,1,0:T(8,128)}, u32[]{:S(2)}) copy-start(f32[2,2,16,2048]{3,2,1,0:T(8,128)} %param.9) | copy-start | bytes 1572868
  7.2 59.0 %all-reduce.26.cloned.1.call-start = ((), (), s32[]{:S(2)}) async-start(), calls=%async_computation.5 | async-start | bytes 786432 | tf_op jit(solution)/shard_map/psum | solution.py:15
  11.2 3.9 copy-start.18
  11.2 3.9 copy-start.19
  15.0 119.4 %all-reduce.24.cloned.1.call-start = ((), (), s32[]{:S(2)}) async-start(), calls=%async_computation.4 | async-start | bytes 1048576 | tf_op jit(solution)/shard_map/psum | solution.py:15
  15.1 0.7 copy-start.28
  72.1 5.5 %copy-start.27 = (f32[3]{0:T(128)S(1)}, f32[3]{0:T(128)}, u32[]{:S(2)}) copy-start(f32[3]{0:T(128)} %constant.149) | copy-start | bytes 40
  72.3 6.2 %collective-permute-start = (f32[3,2,2,1,2048]{4,3,1,2,0:T(1,128)S(1)}, f32[3,2,2,1,2048]{4,3,1,2,0:T(1,128)S(1)}, u32[]{:S(2)}, u32[]{:S(2)}) collective-permute-start(f32[3,2,2,1,2048]{4,3,1,2,0:T(1,128)S(1)} %get-tuple-element.65), channel_id=1, source_target_pairs={{1,0},{2,1},{3,2},{4,3},{5,4},{6,5},{7,6},{8,7},{9,8},{10,9},{11,1... | collective-permute-start | bytes 294920 | tf_op jit(solution)/shard_map/ppermute | solution.py:28
  73.6 5.6 %collective-permute-start.1 = (f32[3,2,2,1,2048]{4,3,1,2,0:T(1,128)S(1)}, f32[3,2,2,1,2048]{4,3,1,2,0:T(1,128)S(1)}, u32[]{:S(2)}, u32[]{:S(2)}) collective-permute-start(f32[3,2,2,1,2048]{4,3,1,2,0:T(1,128)S(1)} %get-tuple-element.66), channel_id=1, source_target_pairs={{0,1},{1,2},{2,3},{3,4},{4,5},{5,6},{6,7},{7,8},{8,9},{9,10},{10,1... | collective-permute-start | bytes 294920 | tf_op jit(solution)/shard_map/ppermute | solution.py:26
  80.6 0.8 copy-start
  80.6 1.5 copy-start.2
  82.1 121.4 %all-reduce.22.cloned.1.call-start = ((), (), s32[]{:S(2)}) async-start(), calls=%async_computation.3 | async-start | bytes 1048576 | tf_op jit(solution)/shard_map/psum | solution.py:15
  134.4 3.0 copy-start.25
  141.4 6.1 %collective-permute-start.2 = (f32[3,2,2,1,2048]{4,3,1,2,0:T(1,128)S(1)}, f32[3,2,2,1,2048]{4,3,1,2,0:T(1,128)S(1)}, u32[]{:S(2)}, u32[]{:S(2)}) collective-permute-start(f32[3,2,2,1,2048]{4,3,1,2,0:T(1,128)S(1)} %get-tuple-element.61), channel_id=1, source_target_pairs={{1,0},{2,1},{3,2},{4,3},{5,4},{6,5},{7,6},{8,7},{9,8},{10,9},{11,1... | collective-permute-start | bytes 294920 | tf_op jit(solution)/shard_map/ppermute | solution.py:28
  142.7 5.6 %collective-permute-start.3 = (f32[3,2,2,1,2048]{4,3,1,2,0:T(1,128)S(1)}, f32[3,2,2,1,2048]{4,3,1,2,0:T(1,128)S(1)}, u32[]{:S(2)}, u32[]{:S(2)}) collective-permute-start(f32[3,2,2,1,2048]{4,3,1,2,0:T(1,128)S(1)} %get-tuple-element.62), channel_id=1, source_target_pairs={{0,1},{1,2},{2,3},{3,4},{4,5},{5,6},{6,7},{7,8},{8,9},{9,10},{10,1... | collective-permute-start | bytes 294920 | tf_op jit(solution)/shard_map/ppermute | solution.py:26
  149.7 0.8 copy-start.4
  149.8 1.5 copy-start.6
  151.3 121.4 %all-reduce.20.cloned.1.call-start = ((), (), s32[]{:S(2)}) async-start(), calls=%async_computation.2 | async-start | bytes 1048576 | tf_op jit(solution)/shard_map/psum | solution.py:15
  203.5 3.0 copy-start.23
  210.5 6.1 %collective-permute-start.4 = (f32[3,2,2,1,2048]{4,3,1,2,0:T(1,128)S(1)}, f32[3,2,2,1,2048]{4,3,1,2,0:T(1,128)S(1)}, u32[]{:S(2)}, u32[]{:S(2)}) collective-permute-start(f32[3,2,2,1,2048]{4,3,1,2,0:T(1,128)S(1)} %get-tuple-element.57), channel_id=1, source_target_pairs={{1,0},{2,1},{3,2},{4,3},{5,4},{6,5},{7,6},{8,7},{9,8},{10,9},{11,1... | collective-permute-start | bytes 294920 | tf_op jit(solution)/shard_map/ppermute | solution.py:28
  211.8 5.6 %collective-permute-start.5 = (f32[3,2,2,1,2048]{4,3,1,2,0:T(1,128)S(1)}, f32[3,2,2,1,2048]{4,3,1,2,0:T(1,128)S(1)}, u32[]{:S(2)}, u32[]{:S(2)}) collective-permute-start(f32[3,2,2,1,2048]{4,3,1,2,0:T(1,128)S(1)} %get-tuple-element.58), channel_id=1, source_target_pairs={{0,1},{1,2},{2,3},{3,4},{4,5},{5,6},{6,7},{7,8},{8,9},{9,10},{10,1... | collective-permute-start | bytes 294920 | tf_op jit(solution)/shard_map/ppermute | solution.py:26
  218.9 0.8 copy-start.8
  218.9 1.5 copy-start.10
  220.4 119.1 %all-reduce.16.cloned.1.call-start = ((), (), s32[]{:S(2)}) async-start(), calls=%async_computation | async-start | bytes 262144 | tf_op jit(solution)/shard_map/psum | solution.py:94
  275.1 0.9 copy-start.16
  275.1 1.0 copy-start.24
  279.1 0.9 copy-start.26
  279.3 6.3 %copy-start.1 = (f32[2,2,16,2048]{3,2,0,1:T(8,128)S(1)}, f32[2,2,16,2048]{3,2,0,1:T(8,128)}, u32[]{:S(2)}) copy-start(f32[2,2,16,2048]{3,2,0,1:T(8,128)} %copy-done) | copy-start | bytes 1572868
  279.3 6.3 %copy-start.3 = (f32[2,2,16,2048]{3,2,0,1:T(8,128)S(1)}, f32[2,2,16,2048]{3,2,0,1:T(8,128)}, u32[]{:S(2)}) copy-start(f32[2,2,16,2048]{3,2,0,1:T(8,128)} %copy-done.2) | copy-start | bytes 1572868
  279.3 6.3 %copy-start.5 = (f32[2,2,16,2048]{3,2,0,1:T(8,128)S(1)}, f32[2,2,16,2048]{3,2,0,1:T(8,128)}, u32[]{:S(2)}) copy-start(f32[2,2,16,2048]{3,2,0,1:T(8,128)} %copy-done.4) | copy-start | bytes 1572868
  279.3 6.3 %copy-start.7 = (f32[2,2,16,2048]{3,2,0,1:T(8,128)S(1)}, f32[2,2,16,2048]{3,2,0,1:T(8,128)}, u32[]{:S(2)}) copy-start(f32[2,2,16,2048]{3,2,0,1:T(8,128)} %copy-done.6) | copy-start | bytes 1572868
  279.3 6.3 %copy-start.12 = (f32[2,2,16,2048]{3,2,0,1:T(8,128)S(1)}, f32[2,2,16,2048]{3,2,0,1:T(8,128)}, u32[]{:S(2)}) copy-start(f32[2,2,16,2048]{3,2,0,1:T(8,128)} %bitcast_add_fusion) | copy-start | bytes 1572868
  279.3 6.3 %copy-start.14 = (f32[2,2,16,2048]{3,2,0,1:T(8,128)S(1)}, f32[2,2,16,2048]{3,2,0,1:T(8,128)}, u32[]{:S(2)}) copy-start(f32[2,2,16,2048]{3,2,0,1:T(8,128)} %bitcast_add_fusion.1) | copy-start | bytes 1572868
  280.1 6.8 %collective-permute-start.6 = (f32[3,2,2,1,2048]{4,3,1,2,0:T(1,128)S(1)}, f32[3,2,2,1,2048]{4,3,1,2,0:T(1,128)S(1)}, u32[]{:S(2)}, u32[]{:S(2)}) collective-permute-start(f32[3,2,2,1,2048]{4,3,1,2,0:T(1,128)S(1)} %get-tuple-element.53), channel_id=1, source_target_pairs={{1,0},{2,1},{3,2},{4,3},{5,4},{6,5},{7,6},{8,7},{9,8},{10,9},{11,1... | collective-permute-start | bytes 294920 | tf_op jit(solution)/shard_map/ppermute | solution.py:28
  281.6 5.6 %collective-permute-start.7 = (f32[3,2,2,1,2048]{4,3,1,2,0:T(1,128)S(1)}, f32[3,2,2,1,2048]{4,3,1,2,0:T(1,128)S(1)}, u32[]{:S(2)}, u32[]{:S(2)}) collective-permute-start(f32[3,2,2,1,2048]{4,3,1,2,0:T(1,128)S(1)} %get-tuple-element.54), channel_id=1, source_target_pairs={{0,1},{1,2},{2,3},{3,4},{4,5},{5,6},{6,7},{7,8},{8,9},{9,10},{10,1... | collective-permute-start | bytes 294920 | tf_op jit(solution)/shard_map/ppermute | solution.py:26
  289.4 51.1 %copy-start.9 = (f32[2,2,16,2048]{3,2,0,1:T(8,128)S(1)}, f32[2,2,16,2048]{3,2,0,1:T(8,128)}, u32[]{:S(2)}) copy-start(f32[2,2,16,2048]{3,2,0,1:T(8,128)} %copy-done.8) | copy-start | bytes 1572868
  289.4 51.1 %copy-start.11 = (f32[2,2,16,2048]{3,2,0,1:T(8,128)S(1)}, f32[2,2,16,2048]{3,2,0,1:T(8,128)}, u32[]{:S(2)}) copy-start(f32[2,2,16,2048]{3,2,0,1:T(8,128)} %copy-done.10) | copy-start | bytes 1572868
  289.4 51.1 %copy-start.13 = (f32[2,2,16,2048]{3,2,0,1:T(8,128)S(1)}, f32[2,2,16,2048]{3,2,0,1:T(8,128)}, u32[]{:S(2)}) copy-start(f32[2,2,16,2048]{3,2,0,1:T(8,128)} %bitcast_add_fusion.2) | copy-start | bytes 1572868
  289.4 109.7 %all-reduce.18.cloned.1.call-start = ((), (), s32[]{:S(2)}) async-start(), calls=%async_computation.1 | async-start | bytes 3145728 | tf_op jit(solution)/shard_map/psum | solution.py:114
  340.5 0.8 copy-start.15
  341.3 4.1 %copy-start.20 = (f32[1,16,2048]{2,1,0:T(8,128)S(1)}, f32[1,16,2048]{2,1,0:T(8,128)}, u32[]{:S(2)}) copy-start(f32[1,16,2048]{2,1,0:T(8,128)} %get-tuple-element.67) | copy-start | bytes 393220
  341.3 4.1 %copy-start.21 = (f32[1,16,2048]{2,1,0:T(8,128)S(1)}, f32[1,16,2048]{2,1,0:T(8,128)}, u32[]{:S(2)}) copy-start(f32[1,16,2048]{2,1,0:T(8,128)} %get-tuple-element.69) | copy-start | bytes 393220
  341.3 4.1 %copy-start.22 = (f32[1,16,2048]{2,1,0:T(8,128)S(1)}, f32[1,16,2048]{2,1,0:T(8,128)}, u32[]{:S(2)}) copy-start(f32[1,16,2048]{2,1,0:T(8,128)} %get-tuple-element.71) | copy-start | bytes 393220
Sparse Core Ops, SparseCore 0:
  15.1 50.9 all-reduce.25
  82.3 52.0 all-reduce.23
  151.4 52.0 all-reduce.21
  220.5 52.0 all-reduce.19
  289.5 49.8 all-reduce.15
  343.0 56.0 all-reduce.17
where the time goes:
time: 409 us; the launch traced here: 408 us
  waiting for transfers between devices  311 us (76%)
  other arithmetic  49.1 us (12%)
  starting transfers between devices  21.7 us (5%)
  between operations  19.8 us (5%)
  local copies, waits for them, and re-layouts  6.24 us (2%)
    psum x4, waiting for transfers between devices, broadcast(): return lax.psum(jnp.where(mine, array, jnp.zeros_like(array)), axis)  205 us
    psum x1, waiting for transfers between devices, body(): summed = lax.psum(grad_terms, 'freq') / freq_count  52.8 us
    psum x1, waiting for transfers between devices, body(): image_depth = lax.psum(partial_image, 'freq') / freq_count  49.2 us
    ppermute x4, starting transfers between devices, extended(): lax.ppermute(tail, axis, [(i, (i + 1) % count) for i in range(ends)])  16.1 us
    sub x3, other arithmetic, body(): real_part = fields[:, :, 0] * cosine - fields[:, :, 1] * sine_val  9.18 us
  transfers between devices with their start and end apart: 14, of which 13 were waited for; matrix products, arithmetic and copies ran while one was open for 1% of the time, Pallas kernels for 0%

commit v1 on v0

v1 whole, which is shorter than its diff:
```python
import functools

import jax
import jax.numpy as jnp
from jax import lax
from jax.experimental import pallas as pl
from jax.experimental.pallas import tpu as pltpu
from jax.sharding import PartitionSpec as P

BASE_FREQ = 2.0
FREQ_STEP = 0.25
DISPERSE = 0.08
DIFFUSE = 0.05
FORCING = 0.5
MESH = pl.DeviceIdType.MESH

PI_HI = 3.140625
PI_LO = 9.67653589793e-4
SIN = (
    1.0,
    -0.16666655242443085,
    0.008333146572113037,
    -0.00019830558449029922,
    2.7278699690214125e-06,
    -2.1673399075439193e-08,
)
COS = (
    1.0,
    -0.4999999701976776,
    0.04166661947965622,
    -0.0013888514367863536,
    2.478722672094591e-05,
    -2.7273267733107787e-07,
    1.805915972319383e-09,
)

STEPS = 4
NF = 4
ROWS = 8
SLABS = 4


def horner(coefs, x):
    total = coefs[-1] * x + coefs[-2]
    for coef in coefs[-3::-1]:
        total = total * x + coef
    return total


def cos_sin(phase):
    t = (phase - PI_HI) - PI_LO
    t2 = t * t
    return -horner(COS, t2), -(t * horner(SIN, t2))


def kernel(
    bands,
    src_hbm,
    rec_hbm,
    adj_hbm,
    slow_hbm,
    eps_hbm,
    del_hbm,
    slab_ref,
    fidx_ref,
    adj_out,
    img_out,
    grad_out,
    sed,
    model,
    msend,
    angb,
    first,
    sr,
    vsr,
    va,
    adj,
    cs,
    row_sr,
    halo_sr,
    row_a,
    halo_a,
    ipart,
    irecv,
    img,
    grad,
    gsend,
    grecv,
    gfin,
    gown,
    gsib,
    local_sem,
    send_sem,
    recv_sem,
):
    ni = sed.shape[-1]
    f = lax.axis_index("freq")
    b = lax.axis_index("xband")
    c = lax.rem(f, 2)
    o = 1 - c
    sib_f = f + 1 - 2 * c
    sib = (sib_f, b)
    far = (lax.rem(f + 2, 4), b)
    farx = (lax.rem(sib_f + 2, 4), b)
    neighbour = (sib_f, lax.rem(b + 2 * c - 1 + bands, bands))

    counts = {"local": 0, "remote": 0}

    def local_copy(source, target):
        k = counts["local"]
        counts["local"] += 1
        copy = pltpu.make_async_copy(source, target, local_sem.at[k])
        copy.start()
        return copy

    def remote_copy(source, target, device):
        k = counts["remote"]
        counts["remote"] += 1
        copy = pltpu.make_async_remote_copy(
            src_ref=source,
            dst_ref=target,
            send_sem=send_sem.at[k],
            recv_sem=recv_sem.at[k],
            device_id=device,
            device_id_type=MESH,
        )
        copy.start()
        return copy

    mine = pl.ds(pl.multiple_of(c * ROWS, ROWS), ROWS)
    theirs = pl.ds(pl.multiple_of(o * ROWS, ROWS), ROWS)
    my_slots = pl.ds(2 * c, 2)
    their_slots = pl.ds(2 * o, 2)

    barrier = pltpu.get_barrier_semaphore()
    for device in (sib, far, farx, neighbour):
        pl.semaphore_signal(barrier, inc=1, device_id=device, device_id_type=MESH)

    loads = [
        local_copy(ref.at[0], sed.at[k]) for k, ref in enumerate((slow_hbm, eps_hbm, del_hbm))
    ]
    fields_hbm = (src_hbm, rec_hbm, adj_hbm)
    own_fields = [
        local_copy(ref.at[:, :, mine], first.at[k, my_slots]) for k, ref in enumerate(fields_hbm)
    ]

    for k in range(2):
        value = BASE_FREQ + FREQ_STEP * fidx_ref[k].astype(jnp.float32)
        angb[2 * c + k] = jnp.full((8, 128), value, jnp.float32)

    for copy in loads:
        copy.wait()
    for rows, ref in ((mine, model.at[f]), (theirs, msend)):
        slow = sed[0, rows]
        ref[0] = slow * (1.0 + sed[1, rows])
        ref[1] = (1.0 + 2.0 * sed[2, rows]) / slow

    pl.semaphore_wait(barrier, 4)
    sends = []
    models = [
        remote_copy(model.at[f], model.at[f], far),
        remote_copy(msend, model.at[f], farx),
        remote_copy(msend, model.at[f], sib),
    ]
    angs = remote_copy(angb.at[my_slots], angb.at[my_slots], sib)
    fields = [
        remote_copy(ref.at[:, :, theirs], first.at[k, my_slots], sib)
        for k, ref in enumerate(fields_hbm)
    ]
    sends += models + [angs] + fields
    for copy in [angs] + models:
        copy.wait_recv()

    slabs = [slab_ref[z] for z in range(STEPS)]
    lanes = lax.broadcasted_iota(jnp.int32, (ROWS, 128), 1)
    sublanes = lax.broadcasted_iota(jnp.int32, (ROWS, ni), 0)
    top_row = sublanes == 0
    last_row = sublanes == ROWS - 1
    keep_top = jnp.where((c == 0) & (b == 0), 0.0, 1.0)
    keep_last = jnp.where((c == 1) & (b == bands - 1), 0.0, 1.0)

    def wide(tile):
        return jnp.concatenate([tile] * (ni // 128), axis=1)

    def trig(z):
        def body(k, carry):
            cosine, sine = cos_sin(wide(angb[k]) * model[slabs[z], 0])
            cs[z, k, 0] = cosine
            cs[z, k, 1] = sine
            return carry

        lax.fori_loop(0, NF, body, 0)

    def rotate(p, q, cosine, sine, sign):
        if sign > 0:
            return p * cosine - q * sine, p * sine + q * cosine
        return p * cosine + q * sine, q * cosine - p * sine

    def put_rows(rows, z, k, j, value):
        rows[z, 0, k, pl.ds(j, 1), :] = value[0:1, :]
        rows[z, 1, k, pl.ds(j, 1), :] = value[ROWS - 1 : ROWS, :]

    def around(v, halos, z, k, j):
        top = halos[z, 0, k, pl.ds(j, 1), :] * keep_top
        last = halos[z, 1, k, pl.ds(j, 1), :] * keep_last
        above = jnp.where(top_row, top, pltpu.roll(v, 1, 0))
        below = jnp.where(last_row, last, pltpu.roll(v, ROWS - 1, 0))
        before = pltpu.roll(v, 1, 1)
        before = jnp.concatenate(
            [jnp.where(lanes == 0, 0.0, before[:, :128]), before[:, 128:]], axis=1
        )
        after = pltpu.roll(v, ni - 1, 1)
        after = jnp.concatenate(
            [after[:, :-128], jnp.where(lanes == 127, 0.0, after[:, -128:])], axis=1
        )
        return (above + below) + (before + after)

    def spread(vr, vi, halos, z, k, j, coupling):
        lap_r = around(vr, halos, z, k, j) - 4.0 * vr
        lap_i = around(vi, halos, z, k, j + 1) - 4.0 * vi
        return (
            vr + DIFFUSE * lap_r - coupling * lap_i,
            vi + DIFFUSE * lap_i + coupling * lap_r,
        )

    def couple(z, k):
        return wide(DISPERSE * BASE_FREQ / angb[k]) * model[slabs[z], 1]

    def rotate_sr(z, k, values):
        cosine, sine = cs[z, k, 0], cs[z, k, 1]
        rotated = rotate(values[0], values[1], cosine, sine, 1) + rotate(
            values[2], values[3], cosine, sine, -1
        )
        for j, value in enumerate(rotated):
            vsr[k, j] = value
            put_rows(row_sr, z, k, j, value)

    def rotate_a(z, k, real, imag):
        rotated = rotate(real, imag, cs[z, k, 0], cs[z, k, 1], -1)
        for j, value in enumerate(rotated):
            va[k, j] = value
            put_rows(row_a, z, k, j, value)

    def send_rows(rows, halos, z):
        return [
            remote_copy(rows.at[z, c], halos.at[z, o], neighbour),
            remote_copy(rows.at[z, o], halos.at[z, c], sib),
        ]

    def first_sr(k, carry):
        rotate_sr(0, k, (first[0, k, 0], first[0, k, 1], first[1, k, 0], first[1, k, 1]))
        return carry

    def first_a(k, carry):
        rotate_a(0, k, first[2, k, 0], first[2, k, 1])
        return carry

    def pass_sr(z):
        def body(k, total):
            coupling = couple(z, k)
            s_r, s_i = spread(vsr[k, 0], vsr[k, 1], halo_sr, z, k, 0, coupling)
            r_r, r_i = spread(vsr[k, 2], vsr[k, 3], halo_sr, z, k, 2, -coupling)
            for j, value in enumerate((s_r, s_i, r_r, r_i)):
                sr[z, k, j] = value
            if z + 1 < STEPS:
                rotate_sr(z + 1, k, (s_r, s_i, r_r, r_i))
            return total + (s_r * r_r + s_i * r_i)

        ipart[z] = lax.fori_loop(0, NF, body, jnp.zeros((ROWS, ni), jnp.float32))

    def pass_a(z):
        def body(k, carry):
            a_r, a_i = spread(va[k, 0], va[k, 1], halo_a, z, k, 0, -couple(z, k))
            adj[k, 0] = a_r
            adj[k, 1] = a_i
            return carry

        lax.fori_loop(0, NF, body, 0)

    def force(z):
        def body(k, totals):
            ang = wide(angb[k])
            inv = wide(BASE_FREQ / angb[k])
            s_r, s_i, r_r, r_i = (sr[z, k, j] for j in range(4))
            half = FORCING * img[z]
            a_r = adj[k, 0] + half * s_r
            a_i = adj[k, 1] + half * s_i
            if z + 1 < STEPS:
                rotate_a(z + 1, k, a_r, a_i)
            else:
                adj[k, 0] = a_r
                adj[k, 1] = a_i
            grad[z, 0] = jnp.where(k == 0, 0.0, grad[z, 0]) + ang * (s_r * a_i - s_i * a_r)
            grad[z, 1] = jnp.where(k == 0, 0.0, grad[z, 1]) + ang * (r_r * a_i - r_i * a_r)
            grad[z, 2] = jnp.where(k == 0, 0.0, grad[z, 2]) + inv * (s_r * a_r + s_i * a_i)
            return totals

        lax.fori_loop(0, NF, body, 0)

    trig(0)
    for copy in own_fields[:2]:
        copy.wait()
    for copy in fields[:2]:
        copy.wait_recv()
    lax.fori_loop(0, NF, first_sr, 0)
    wait_sr = send_rows(row_sr, halo_sr, 0)
    own_fields[2].wait()
    fields[2].wait_recv()
    lax.fori_loop(0, NF, first_a, 0)
    wait_a = send_rows(row_a, halo_a, 0)
    sends += wait_sr + wait_a
    trig(1)

    def uses(chip):
        at = []
        for j in range(2):
            step = 0
            for z in range(1, STEPS):
                step = jnp.where(slabs[z] == 2 * chip + j, z, step)
            at.append(step)
        return jnp.minimum(at[0], at[1]), jnp.maximum(at[0], at[1]), at[0] < at[1]

    chip = f // 2
    far_uses = uses(1 - chip)
    my_uses = uses(chip)
    copies = []
    arrivals = []
    gradients = []

    for z in range(STEPS):
        for copy in wait_sr:
            copy.wait_recv()
        pass_sr(z)
        if z + 1 < STEPS:
            wait_sr = send_rows(row_sr, halo_sr, z + 1)
            sends += wait_sr
        image = remote_copy(ipart.at[z], irecv.at[z], far)
        sends.append(image)
        if z + 2 < STEPS:
            trig(z + 2)
        for copy in wait_a:
            copy.wait_recv()
        pass_a(z)
        image.wait_recv()
        img[z] = (ipart[z] + irecv[z]) * (1.0 / (2 * NF))
        force(z)
        if z + 1 < STEPS:
            wait_a = send_rows(row_a, halo_a, z + 1)
            sends += wait_a
        else:
            arrivals.append(remote_copy(adj.at[their_slots], adj_out.at[:, :, mine], sib))
            copies.append(local_copy(adj.at[my_slots], adj_out.at[:, :, mine]))
        if z >= STEPS - 2:
            n = z - (STEPS - 2)
            for j in range(3):
                gsend[n, j] = grad[far_uses[n], j]
            gradients.append(remote_copy(gsend.at[n], grecv.at[n], far))
        copies.append(local_copy(img.at[z], img_out.at[z, mine]))
        arrivals.append(remote_copy(img.at[z], img_out.at[z, mine], sib))
    sends += gradients

    for n in range(2):
        gradients[n].wait_recv()
        for j in range(3):
            gfin[n, j] = (grad[my_uses[n], j] + grecv[n, j]) * (1.0 / (2 * NF))
    first_is_zero = my_uses[2].astype(jnp.int32)
    own_is = jnp.where(c == 0, 1 - first_is_zero, first_is_zero)
    for j in range(3):
        gsib[j] = gfin[1 - own_is, j]
    arrivals.append(remote_copy(gsib, grad_out.at[0, :, mine], sib))
    for j in range(3):
        gown[j] = gfin[own_is, j]
    copies.append(local_copy(gown, grad_out.at[0, :, mine]))
    for copy in arrivals:
        copy.wait_recv()
    for copy in copies:
        copy.wait()
    for copy in sends + arrivals:
        copy.wait_send()


def solution(mesh):
    bands = mesh.shape["xband"]

    def step(*args):
        ni = args[0].shape[-1]
        half = (ROWS, ni)
        f32 = jnp.float32

        def vmem(*shape):
            return pltpu.VMEM(shape, f32)

        scratch = [
            vmem(3, 2 * ROWS, ni),
            vmem(SLABS, 2, *half),
            vmem(2, *half),
            vmem(NF, 8, 128),
            vmem(3, NF, 2, *half),
            vmem(STEPS, NF, 4, *half),
            vmem(NF, 4, *half),
            vmem(NF, 2, *half),
            vmem(NF, 2, *half),
            vmem(STEPS, NF, 2, *half),
            vmem(STEPS, 2, NF, 4, ni),
            vmem(STEPS, 2, NF, 4, ni),
            vmem(STEPS, 2, NF, 2, ni),
            vmem(STEPS, 2, NF, 2, ni),
            vmem(STEPS, *half),
            vmem(STEPS, *half),
            vmem(STEPS, *half),
            vmem(STEPS, 3, *half),
            vmem(2, 3, *half),
            vmem(2, 3, *half),
            vmem(2, 3, *half),
            vmem(3, *half),
            vmem(3, *half),
            pltpu.SemaphoreType.DMA((16,)),
            pltpu.SemaphoreType.DMA((40,)),
            pltpu.SemaphoreType.DMA((40,)),
        ]
        any_spec = pl.BlockSpec(memory_space=pl.ANY)
        smem_spec = pl.BlockSpec(memory_space=pltpu.SMEM)
        return pl.pallas_call(
            functools.partial(kernel, bands),
            out_shape=(
                jax.ShapeDtypeStruct(args[2].shape, f32),
                jax.ShapeDtypeStruct((STEPS,) + args[3].shape[1:], f32),
                jax.ShapeDtypeStruct((1, 3) + args[3].shape[1:], f32),
            ),
            in_specs=[any_spec] * 6 + [smem_spec] * 2,
            out_specs=(any_spec,) * 3,
            scratch_shapes=scratch,
            compiler_params=pltpu.CompilerParams(
                collective_id=0, has_side_effects=True, vmem_limit_bytes=40 * 2**20
            ),
        )(*args)

    return jax.shard_map(
        step,
        mesh=mesh,
        in_specs=(
            P("freq", None, "xband", None),
            P("freq", None, "xband", None),
            P("freq", None, "xband", None),
            P("freq", "xband", None),
            P("freq", "xband", None),
            P("freq", "xband", None),
            P(),
            P("freq"),
        ),
        out_specs=(
            P("freq", None, "xband", None),
            P(None, "xband", None),
            P("freq", None, "xband", None),
        ),
        check_vma=False,
    )
```

time: 409 us -> 74.7 us (0.18)
  the two profiles are of different devices: /device:TPU:1 before, /device:TPU:31 now
where the time goes in v1:
time: 74.7 us; the launch traced here: 74.4 us
  Pallas kernels  64.3 us (86%)
  local copies, waits for them, and re-layouts  9.47 us (13%)
    pallas_call x1, Pallas kernels, step(): pl.pallas_call(functools.partial(kernel, bands), out_shape=(jax.ShapeDtyp...  64.3 us
    unnamed x19, local copies, waits for them, and re-layouts  9.47 us

profile of v1, /device:TPU:31, one launch (start us, length us, event | category | flops | bytes accessed | tf_op | source)
XLA Modules:
  0.0 74.4 jit_solution(398016240391864335)
XLA Ops:
  0.6 0.0 copy-start
  0.6 1.0 %copy-done = f32[2,2,16,2048]{3,2,1,0:T(8,128)S(1)} copy-done((f32[2,2,16,2048]{3,2,1,0:T(8,128)S(1)}, f32[2,2,16,2048]{3,2,1,0:T(8,128)}, u32[]{:S(2)}) %copy-start) | copy-done | bytes 524312
  1.7 0.0 copy-start.1
  1.7 1.0 %copy-done.1 = f32[2,2,16,2048]{3,2,1,0:T(8,128)S(1)} copy-done((f32[2,2,16,2048]{3,2,1,0:T(8,128)S(1)}, f32[2,2,16,2048]{3,2,1,0:T(8,128)}, u32[]{:S(2)}) %copy-start.1) | copy-done | bytes 524312
  2.7 0.0 copy-start.2
  2.7 1.0 %copy-done.2 = f32[2,2,16,2048]{3,2,1,0:T(8,128)S(1)} copy-done((f32[2,2,16,2048]{3,2,1,0:T(8,128)S(1)}, f32[2,2,16,2048]{3,2,1,0:T(8,128)}, u32[]{:S(2)}) %copy-start.2) | copy-done | bytes 524312
  3.8 0.0 copy-start.3
  3.8 0.9 %copy-done.3 = f32[1,16,2048]{2,1,0:T(8,128)S(1)} copy-done((f32[1,16,2048]{2,1,0:T(8,128)S(1)}, f32[1,16,2048]{2,1,0:T(8,128)}, u32[]{:S(2)}) %copy-start.3) | copy-done | bytes 131096
  4.7 0.0 copy-start.4
  4.7 0.9 %copy-done.4 = f32[1,16,2048]{2,1,0:T(8,128)S(1)} copy-done((f32[1,16,2048]{2,1,0:T(8,128)S(1)}, f32[1,16,2048]{2,1,0:T(8,128)}, u32[]{:S(2)}) %copy-start.4) | copy-done | bytes 131096
  5.6 0.0 copy-start.5
  5.6 0.9 %copy-done.5 = f32[1,16,2048]{2,1,0:T(8,128)S(1)} copy-done((f32[1,16,2048]{2,1,0:T(8,128)S(1)}, f32[1,16,2048]{2,1,0:T(8,128)}, u32[]{:S(2)}) %copy-start.5) | copy-done | bytes 131096
  6.5 0.0 copy-start.6
  6.5 0.7 copy-done.6
  7.1 0.0 copy-start.7
  7.1 0.7 copy-done.7
  7.8 64.3 %shard_map.103 = (f32[2,2,16,2048]{3,2,1,0:T(8,128)S(1)}, f32[4,16,2048]{2,1,0:T(8,128)S(1)}, f32[1,3,16,2048]{3,2,1,0:T(8,128)S(1)}) custom-call(f32[2,2,16,2048]{3,2,1,0:T(8,128)S(1)} %copy-done, f32[2,2,16,2048]{3,2,1,0:T(8,128)S(1)} %copy-done.1, f32[2,2,16,2048]{3,2,1,0:T(8,128)S(1)} %copy-done.2, f32[1,16,2048]{2,1,0:T(8,128)S(1)} %copy-done.3, ...), custom_call_target="tpu_custom_call" | custom-call | tf_op jit(solution)/shard_map/pallas_call | solution.py:423
  72.1 0.8 %copy.14 = f32[2,2,16,2048]{3,2,1,0:T(8,128)} copy(f32[2,2,16,2048]{3,2,1,0:T(8,128)S(1)} %get-tuple-element.6) | data formatting | bytes 1048576
  72.9 0.8 %copy.15 = f32[4,16,2048]{2,1,0:T(8,128)} copy(f32[4,16,2048]{2,1,0:T(8,128)S(1)} %get-tuple-element.7) | data formatting | bytes 1048576
  73.7 0.7 %copy.16 = f32[1,3,16,2048]{3,2,1,0:T(8,128)} copy(f32[1,3,16,2048]{3,2,1,0:T(8,128)S(1)} %get-tuple-element.8) | data formatting | bytes 786432
Async XLA Ops:
  0.6 1.0 %copy-start = (f32[2,2,16,2048]{3,2,1,0:T(8,128)S(1)}, f32[2,2,16,2048]{3,2,1,0:T(8,128)}, u32[]{:S(2)}) copy-start(f32[2,2,16,2048]{3,2,1,0:T(8,128)} %src_hbm.1) | copy-start | bytes 1572868
  1.7 1.0 %copy-start.1 = (f32[2,2,16,2048]{3,2,1,0:T(8,128)S(1)}, f32[2,2,16,2048]{3,2,1,0:T(8,128)}, u32[]{:S(2)}) copy-start(f32[2,2,16,2048]{3,2,1,0:T(8,128)} %rec_hbm.1) | copy-start | bytes 1572868
  2.7 1.0 %copy-start.2 = (f32[2,2,16,2048]{3,2,1,0:T(8,128)S(1)}, f32[2,2,16,2048]{3,2,1,0:T(8,128)}, u32[]{:S(2)}) copy-start(f32[2,2,16,2048]{3,2,1,0:T(8,128)} %adj_hbm.1) | copy-start | bytes 1572868
  3.8 0.9 %copy-start.3 = (f32[1,16,2048]{2,1,0:T(8,128)S(1)}, f32[1,16,2048]{2,1,0:T(8,128)}, u32[]{:S(2)}) copy-start(f32[1,16,2048]{2,1,0:T(8,128)} %slow_hbm.1) | copy-start | bytes 393220
  4.7 0.9 %copy-start.4 = (f32[1,16,2048]{2,1,0:T(8,128)S(1)}, f32[1,16,2048]{2,1,0:T(8,128)}, u32[]{:S(2)}) copy-start(f32[1,16,2048]{2,1,0:T(8,128)} %eps_hbm.1) | copy-start | bytes 393220
  5.6 0.9 %copy-start.5 = (f32[1,16,2048]{2,1,0:T(8,128)S(1)}, f32[1,16,2048]{2,1,0:T(8,128)}, u32[]{:S(2)}) copy-start(f32[1,16,2048]{2,1,0:T(8,128)} %del_hbm.1) | copy-start | bytes 393220
  6.5 0.7 copy-start.6
  7.1 0.7 copy-start.7

commit v2 on v1

--- a/solution.py
+++ b/solution.py
@@ -38,6 +38,7 @@
 NF = 4
 ROWS = 8
 SLABS = 4
+LAG = 1
 
 
 def horner(coefs, x):
@@ -61,8 +62,8 @@
     slow_hbm,
     eps_hbm,
     del_hbm,
-    slab_ref,
-    fidx_ref,
+    slab_hbm,
+    fidx_hbm,
     adj_out,
     img_out,
     grad_out,
@@ -89,9 +90,22 @@
     gfin,
     gown,
     gsib,
+    slab_ref,
+    fidx_ref,
+    stage,
+    edge_send,
+    edge_recv,
+    slow_send,
+    slow_recv,
     local_sem,
     send_sem,
     recv_sem,
+    sr_send_sem,
+    sr_recv_sem,
+    edge_send_sem,
+    edge_recv_sem,
+    slow_send_sem,
+    slow_recv_sem,
 ):
     ni = sed.shape[-1]
     f = lax.axis_index("freq")
@@ -132,18 +146,25 @@
     my_slots = pl.ds(2 * c, 2)
     their_slots = pl.ds(2 * o, 2)
 
+    outer_band = lax.rem(b + 2 * c - 1 + bands, bands)
+    after_band = lax.rem(b + 1, bands)
+    before_band = lax.rem(b + bands - 1, bands)
+    chip = f // 2
     barrier = pltpu.get_barrier_semaphore()
-    for device in (sib, far, farx, neighbour):
+    for device in [sib, far, farx] + [(k, outer_band) for k in range(4)]:
         pl.semaphore_signal(barrier, inc=1, device_id=device, device_id_type=MESH)
 
+    ints = [local_copy(fidx_hbm, fidx_ref), local_copy(slab_hbm, slab_ref)]
     loads = [
         local_copy(ref.at[0], sed.at[k]) for k, ref in enumerate((slow_hbm, eps_hbm, del_hbm))
     ]
     fields_hbm = (src_hbm, rec_hbm, adj_hbm)
+    stages = [local_copy(ref, stage.at[k]) for k, ref in enumerate(fields_hbm[:2])]
     own_fields = [
         local_copy(ref.at[:, :, mine], first.at[k, my_slots]) for k, ref in enumerate(fields_hbm)
     ]
 
+    ints[0].wait()
     for k in range(2):
         value = BASE_FREQ + FREQ_STEP * fidx_ref[k].astype(jnp.float32)
         angb[2 * c + k] = jnp.full((8, 128), value, jnp.float32)
@@ -154,23 +175,66 @@
         slow = sed[0, rows]
         ref[0] = slow * (1.0 + sed[1, rows])
         ref[1] = (1.0 + 2.0 * sed[2, rows]) / slow
-
-    pl.semaphore_wait(barrier, 4)
+    for side, row in ((0, 0), (1, 2 * ROWS - 1)):
+        slow_send[side] = sed[0, row : row + 1] * (1.0 + sed[1, row : row + 1])
+    def edge_copy(side, sender, device):
+        return pltpu.make_async_remote_copy(
+            src_ref=edge_send.at[side],
+            dst_ref=edge_recv.at[sender],
+            send_sem=edge_send_sem.at[side],
+            recv_sem=edge_recv_sem.at[sender],
+            device_id=device,
+            device_id_type=MESH,
+        )
+
+    def slow_copy(n, sender, device):
+        return pltpu.make_async_remote_copy(
+            src_ref=slow_send.at[n // 2],
+            dst_ref=slow_recv.at[sender],
+            send_sem=slow_send_sem.at[n],
+            recv_sem=slow_recv_sem.at[sender],
+            device_id=device,
+            device_id_type=MESH,
+        )
+
+    pl.semaphore_wait(barrier, 7)
     sends = []
     models = [
         remote_copy(model.at[f], model.at[f], far),
         remote_copy(msend, model.at[f], farx),
         remote_copy(msend, model.at[f], sib),
     ]
+    early = [
+        edge_copy(0, c, (2 * chip + 1, before_band)),
+        edge_copy(1, c, (2 * chip, after_band)),
+        slow_copy(0, f, (1, before_band)),
+        slow_copy(1, f, (3, before_band)),
+        slow_copy(2, f, (0, after_band)),
+        slow_copy(3, f, (2, after_band)),
+    ]
+    for copy in early[2:]:
+        copy.start()
+    for copy in stages:
+        copy.wait()
+    for side, row in ((0, 0), (1, 2 * ROWS - 1)):
+        for field in range(2):
+            for k in range(2):
+                for part in range(2):
+                    at = 2 * field + k
+                    edge_send[side, part, at : at + 1] = stage[field, k, part, row : row + 1]
+
+    for copy in early[:2]:
+        copy.start()
     angs = remote_copy(angb.at[my_slots], angb.at[my_slots], sib)
     fields = [
         remote_copy(ref.at[:, :, theirs], first.at[k, my_slots], sib)
         for k, ref in enumerate(fields_hbm)
     ]
-    sends += models + [angs] + fields
+    sends += models + [angs] + fields + early
     for copy in [angs] + models:
         copy.wait_recv()
 
+    ints[1].wait()
     slabs = [slab_ref[z] for z in range(STEPS)]
     lanes = lax.broadcasted_iota(jnp.int32, (ROWS, 128), 1)
     sublanes = lax.broadcasted_iota(jnp.int32, (ROWS, ni), 0)
@@ -247,8 +311,48 @@
             remote_copy(rows.at[z, o], halos.at[z, c], sib),
         ]
 
+    def sr_outer(z, k):
+        return pltpu.make_async_remote_copy(
+            src_ref=row_sr.at[z, c, k],
+            dst_ref=halo_sr.at[z, o, k],
+            send_sem=sr_send_sem.at[z, k, 0],
+            recv_sem=sr_recv_sem.at[z, k, 0],
+            device_id=neighbour,
+            device_id_type=MESH,
+        )
+
+    def sr_inner(z, k):
+        return pltpu.make_async_remote_copy(
+            src_ref=row_sr.at[z, o, k],
+            dst_ref=halo_sr.at[z, c, k],
+            send_sem=sr_send_sem.at[z, k, 1],
+            recv_sem=sr_recv_sem.at[z, k, 1],
+            device_id=sib,
+            device_id_type=MESH,
+        )
+
+    def first_edges():
+        slow_row = slow_recv[slabs[0]]
+        rows4 = lax.broadcasted_iota(jnp.int32, (4, ni), 0)
+        for core in range(2):
+            tile = jnp.where(
+                lax.broadcasted_iota(jnp.int32, (4, 128), 0) % 2 == 0,
+                angb[2 * core, 0:4],
+                angb[2 * core + 1, 0:4],
+            )
+            cosine, sine = cos_sin(wide(tile) * slow_row)
+            sine = jnp.where(rows4 < 2, sine, -sine)
+            p, q = edge_recv[core, 0], edge_recv[core, 1]
+            real, imag = p * cosine - q * sine, p * sine + q * cosine
+            for field in range(2):
+                for k in range(2):
+                    at = 2 * field + k
+                    halo_sr[0, c, 2 * core + k, 2 * field : 2 * field + 1] = real[at : at + 1]
+                    halo_sr[0, c, 2 * core + k, 2 * field + 1 : 2 * field + 2] = imag[at : at + 1]
+
     def first_sr(k, carry):
         rotate_sr(0, k, (first[0, k, 0], first[0, k, 1], first[1, k, 0], first[1, k, 1]))
+        sr_inner(0, k).start()
         return carry
 
     def first_a(k, carry):
@@ -258,12 +362,17 @@
     def pass_sr(z):
         def body(k, total):
             coupling = couple(z, k)
+            if z > 0:
+                sr_outer(z, k).wait_recv()
+            sr_inner(z, k).wait_recv()
             s_r, s_i = spread(vsr[k, 0], vsr[k, 1], halo_sr, z, k, 0, coupling)
             r_r, r_i = spread(vsr[k, 2], vsr[k, 3], halo_sr, z, k, 2, -coupling)
             for j, value in enumerate((s_r, s_i, r_r, r_i)):
                 sr[z, k, j] = value
             if z + 1 < STEPS:
                 rotate_sr(z + 1, k, (s_r, s_i, r_r, r_i))
+                sr_outer(z + 1, k).start()
+                sr_inner(z + 1, k).start()
             return total + (s_r * r_r + s_i * r_i)
 
         ipart[z] = lax.fori_loop(0, NF, body, jnp.zeros((ROWS, ni), jnp.float32))
@@ -303,12 +412,11 @@
     for copy in fields[:2]:
         copy.wait_recv()
     lax.fori_loop(0, NF, first_sr, 0)
-    wait_sr = send_rows(row_sr, halo_sr, 0)
-    own_fields[2].wait()
-    fields[2].wait_recv()
-    lax.fori_loop(0, NF, first_a, 0)
-    wait_a = send_rows(row_a, halo_a, 0)
-    sends += wait_sr + wait_a
+    for core in range(2):
+        edge_copy(0, core, sib).wait_recv()
+    for k in range(SLABS):
+        slow_copy(0, k, sib).wait_recv()
+    first_edges()
     trig(1)
 
     def uses(chip):
@@ -320,69 +428,94 @@
             at.append(step)
         return jnp.minimum(at[0], at[1]), jnp.maximum(at[0], at[1]), at[0] < at[1]
 
-    chip = f // 2
     far_uses = uses(1 - chip)
     my_uses = uses(chip)
     copies = []
     arrivals = []
     gradients = []
 
-    for z in range(STEPS):
-        for copy in wait_sr:
-            copy.wait_recv()
-        pass_sr(z)
-        if z + 1 < STEPS:
-            wait_sr = send_rows(row_sr, halo_sr, z + 1)
-            sends += wait_sr
-        image = remote_copy(ipart.at[z], irecv.at[z], far)
-        sends.append(image)
-        if z + 2 < STEPS:
-            trig(z + 2)
+    def finish(z, wait_a, image):
         for copy in wait_a:
             copy.wait_recv()
         pass_a(z)
         image.wait_recv()
         img[z] = (ipart[z] + irecv[z]) * (1.0 / (2 * NF))
         force(z)
+        wait_a = []
         if z + 1 < STEPS:
             wait_a = send_rows(row_a, halo_a, z + 1)
-            sends += wait_a
-        else:
-            arrivals.append(remote_copy(adj.at[their_slots], adj_out.at[:, :, mine], sib))
-            copies.append(local_copy(adj.at[my_slots], adj_out.at[:, :, mine]))
+            sends.extend(wait_a)
         if z >= STEPS - 2:
             n = z - (STEPS - 2)
             for j in range(3):
                 gsend[n, j] = grad[far_uses[n], j]
-            gradients.append(remote_copy(gsend.at[n], grecv.at[n], far))
+                gradients.append(remote_copy(gsend.at[n, j], grecv.at[n, j], far))
+        if z + 1 == STEPS:
+            arrivals.append(remote_copy(adj.at[their_slots], adj_out.at[:, :, mine], sib))
+            copies.append(local_copy(adj.at[my_slots], adj_out.at[:, :, mine]))
         copies.append(local_copy(img.at[z], img_out.at[z, mine]))
         arrivals.append(remote_copy(img.at[z], img_out.at[z, mine], sib))
+        return wait_a
+
+    images = []
+    for z in range(STEPS):
+        pass_sr(z)
+        images.append(remote_copy(ipart.at[z], irecv.at[z], far))
+        if z == 0:
+            own_fields[2].wait()
+            fields[2].wait_recv()
+            lax.fori_loop(0, NF, first_a, 0)
+            wait_a = send_rows(row_a, halo_a, 0)
+            sends += wait_a
+        if z + 2 < STEPS:
+            trig(z + 2)
+        if LAG == 0:
+            wait_a = finish(z, wait_a, images[z])
+        elif z > 0:
+            wait_a = finish(z - 1, wait_a, images[z - 1])
+    if LAG:
+        wait_a = finish(STEPS - 1, wait_a, images[STEPS - 1])
+    sends += images
     sends += gradients
 
-    for n in range(2):
-        gradients[n].wait_recv()
-        for j in range(3):
-            gfin[n, j] = (grad[my_uses[n], j] + grecv[n, j]) * (1.0 / (2 * NF))
     first_is_zero = my_uses[2].astype(jnp.int32)
     own_is = jnp.where(c == 0, 1 - first_is_zero, first_is_zero)
     for j in range(3):
+        for n in range(2):
+            gradients[3 * n + j].wait_recv()
+            gfin[n, j] = (grad[my_uses[n], j] + grecv[n, j]) * (1.0 / (2 * NF))
         gsib[j] = gfin[1 - own_is, j]
-    arrivals.append(remote_copy(gsib, grad_out.at[0, :, mine], sib))
-    for j in range(3):
+        arrivals.append(remote_copy(gsib.at[j], grad_out.at[0, j, mine], sib))
         gown[j] = gfin[own_is, j]
-    copies.append(local_copy(gown, grad_out.at[0, :, mine]))
+        copies.append(local_copy(gown.at[j], grad_out.at[0, j, mine]))
     for copy in arrivals:
         copy.wait_recv()
     for copy in copies:
         copy.wait()
     for copy in sends + arrivals:
         copy.wait_send()
+    for z in range(STEPS):
+        for k in range(NF):
+            if z > 0:
+                sr_outer(z, k).wait_send()
+            sr_inner(z, k).wait_send()
+
+
+def hand_over(*refs):
+    copies = [
+        pltpu.make_async_copy(refs[k], refs[3 + k], refs[6].at[k]) for k in range(3)
+    ]
+    for copy in copies:
+        copy.start()
+    for copy in copies:
+        copy.wait()
 
 
 def solution(mesh):
     bands = mesh.shape["xband"]
 
     def step(*args):
+        args = [pltpu.with_memory_space_constraint(x, pltpu.HBM) for x in args]
         ni = args[0].shape[-1]
         half = (ROWS, ni)
         f32 = jnp.float32
@@ -414,26 +547,47 @@
             vmem(2, 3, *half),
             vmem(3, *half),
             vmem(3, *half),
-            pltpu.SemaphoreType.DMA((16,)),
+            pltpu.SMEM(args[6].shape, jnp.int32),
+            pltpu.SMEM(args[7].shape, jnp.int32),
+            vmem(2, 2, 2, 2 * ROWS, ni),
+            vmem(2, 2, 4, ni),
+            vmem(2, 2, 4, ni),
+            vmem(2, 1, ni),
+            vmem(SLABS, 1, ni),
+            pltpu.SemaphoreType.DMA((24,)),
             pltpu.SemaphoreType.DMA((40,)),
             pltpu.SemaphoreType.DMA((40,)),
+            pltpu.SemaphoreType.DMA((STEPS, NF, 2)),
+            pltpu.SemaphoreType.DMA((STEPS, NF, 2)),
+            pltpu.SemaphoreType.DMA((2,)),
+            pltpu.SemaphoreType.DMA((2,)),
+            pltpu.SemaphoreType.DMA((4,)),
+            pltpu.SemaphoreType.DMA((SLABS,)),
         ]
         any_spec = pl.BlockSpec(memory_space=pl.ANY)
-        smem_spec = pl.BlockSpec(memory_space=pltpu.SMEM)
-        return pl.pallas_call(
+        hbm_spec = pl.BlockSpec(memory_space=pltpu.HBM)
+        outs = pl.pallas_call(
             functools.partial(kernel, bands),
             out_shape=(
                 jax.ShapeDtypeStruct(args[2].shape, f32),
                 jax.ShapeDtypeStruct((STEPS,) + args[3].shape[1:], f32),
                 jax.ShapeDtypeStruct((1, 3) + args[3].shape[1:], f32),
             ),
-            in_specs=[any_spec] * 6 + [smem_spec] * 2,
+            in_specs=[hbm_spec] * 8,
             out_specs=(any_spec,) * 3,
             scratch_shapes=scratch,
             compiler_params=pltpu.CompilerParams(
                 collective_id=0, has_side_effects=True, vmem_limit_bytes=40 * 2**20
             ),
         )(*args)
+        return pl.pallas_call(
+            hand_over,
+            out_shape=tuple(jax.ShapeDtypeStruct(x.shape, f32) for x in outs),
+            in_specs=[any_spec] * 3,
+            out_specs=(any_spec,) * 3,
+            scratch_shapes=[pltpu.SemaphoreType.DMA((3,))],
+            compiler_params=pltpu.CompilerParams(vmem_limit_bytes=4 * 2**20),
+        )(*outs)
 
     return jax.shard_map(
         step,

time: 74.7 us -> 58.7 us (0.79)
  the two profiles are of different devices: /device:TPU:31 before, /device:TPU:1 now
where the time goes in v2:
time: 58.7 us; the launch traced here: 58.6 us
  Pallas kernels  58 us (99%)
  between operations  0.64 us (1%)
    pallas_call x1, Pallas kernels, step(): pl.pallas_call(functools.partial(kernel, bands), out_shape=(jax.ShapeDtyp...  56.9 us

profile of v2, /device:TPU:1, one launch (start us, length us, event | category | flops | bytes accessed | tf_op | source)
XLA Modules:
  0.0 58.6 jit_solution(2659832180708668193)
XLA Ops:
  0.6 56.9 %shard_map.103 = (f32[2,2,16,2048]{3,2,1,0:T(8,128)S(1)}, f32[4,16,2048]{2,1,0:T(8,128)S(1)}, f32[1,3,16,2048]{3,2,1,0:T(8,128)S(1)}) custom-call(f32[2,2,16,2048]{3,2,1,0:T(8,128)} %src_hbm.1, f32[2,2,16,2048]{3,2,1,0:T(8,128)} %rec_hbm.1, f32[2,2,16,2048]{3,2,1,0:T(8,128)} %adj_hbm.1, f32[1,16,2048]{2,1,0:T(8,128)} %slow_hbm.1, f32[1,16,2048]{2,1,0:T(8,128)} %eps_hbm.1, ...), custom_call_target="tpu_custom_call" | custom-call | tf_op jit(solution)/shard_map/pallas_call | solution.py:569
  57.5 1.1 %shard_map.104 = (f32[2,2,16,2048]{3,2,1,0:T(8,128)}, f32[4,16,2048]{2,1,0:T(8,128)}, f32[1,3,16,2048]{3,2,1,0:T(8,128)}) custom-call(f32[2,2,16,2048]{3,2,1,0:T(8,128)S(1)} %get-tuple-element.6.refs_0_, f32[4,16,2048]{2,1,0:T(8,128)S(1)} %get-tuple-element.7.refs_1_, f32[1,3,16,2048]{3,2,1,0:T(8,128)S(1)} %get-tuple-element.8.refs_2_), custom_call_target="tpu_custom_call" | custom-call | tf_op jit(solution)/shard_map/pallas_call | solution.py:583

commit v3 on v2

--- a/solution.py
+++ b/solution.py
@@ -95,6 +95,10 @@
     stage,
     edge_send,
     edge_recv,
+    edge_a_send,
+    edge_a_recv,
+    edge_raw,
+    edge_near,
     slow_send,
     slow_recv,
     local_sem,
@@ -104,6 +108,8 @@
     sr_recv_sem,
     edge_send_sem,
     edge_recv_sem,
+    edge_a_send_sem,
+    edge_a_recv_sem,
     slow_send_sem,
     slow_recv_sem,
 ):
@@ -159,7 +165,7 @@
         local_copy(ref.at[0], sed.at[k]) for k, ref in enumerate((slow_hbm, eps_hbm, del_hbm))
     ]
     fields_hbm = (src_hbm, rec_hbm, adj_hbm)
-    stages = [local_copy(ref, stage.at[k]) for k, ref in enumerate(fields_hbm[:2])]
+    stages = [local_copy(ref, stage.at[k]) for k, ref in enumerate(fields_hbm)]
     own_fields = [
         local_copy(ref.at[:, :, mine], first.at[k, my_slots]) for k, ref in enumerate(fields_hbm)
     ]
@@ -175,14 +181,26 @@
         slow = sed[0, rows]
         ref[0] = slow * (1.0 + sed[1, rows])
         ref[1] = (1.0 + 2.0 * sed[2, rows]) / slow
-    for side, row in ((0, 0), (1, 2 * ROWS - 1)):
-        slow_send[side] = sed[0, row : row + 1] * (1.0 + sed[1, row : row + 1])
-    def edge_copy(side, sender, device):
+    for side, near, second in ((0, 0, 1), (1, 2 * ROWS - 1, 2 * ROWS - 2)):
+        for n, row in enumerate((near, second)):
+            slow_send[side, n] = sed[0, row : row + 1] * (1.0 + sed[1, row : row + 1])
+        slow_send[side, 2] = (1.0 + 2.0 * sed[2, near : near + 1]) / sed[0, near : near + 1]
+    def edge_copy(side, n, sender, device):
         return pltpu.make_async_remote_copy(
-            src_ref=edge_send.at[side],
-            dst_ref=edge_recv.at[sender],
-            send_sem=edge_send_sem.at[side],
-            recv_sem=edge_recv_sem.at[sender],
+            src_ref=edge_send.at[side, n],
+            dst_ref=edge_recv.at[sender, n],
+            send_sem=edge_send_sem.at[side, n],
+            recv_sem=edge_recv_sem.at[sender, n],
+            device_id=device,
+            device_id_type=MESH,
+        )
+
+    def edge_a_copy(side, sender, device):
+        return pltpu.make_async_remote_copy(
+            src_ref=edge_a_send.at[side],
+            dst_ref=edge_a_recv.at[sender],
+            send_sem=edge_a_send_sem.at[side],
+            recv_sem=edge_a_recv_sem.at[sender],
             device_id=device,
             device_id_type=MESH,
         )
@@ -204,33 +222,52 @@
         remote_copy(msend, model.at[f], farx),
         remote_copy(msend, model.at[f], sib),
     ]
-    early = [
-        edge_copy(0, c, (2 * chip + 1, before_band)),
-        edge_copy(1, c, (2 * chip, after_band)),
+    before, after = (2 * chip + 1, before_band), (2 * chip, after_band)
+    slows = [
         slow_copy(0, f, (1, before_band)),
         slow_copy(1, f, (3, before_band)),
         slow_copy(2, f, (0, after_band)),
         slow_copy(3, f, (2, after_band)),
     ]
-    for copy in early[2:]:
+    nears = [edge_copy(0, 0, c, before), edge_copy(1, 0, c, after)]
+    seconds = [
+        edge_a_copy(0, c, before),
+        edge_a_copy(1, c, after),
+        edge_copy(0, 1, c, before),
+        edge_copy(1, 1, c, after),
+    ]
+    for copy in slows:
         copy.start()
     for copy in stages:
         copy.wait()
-    for side, row in ((0, 0), (1, 2 * ROWS - 1)):
-        for field in range(2):
-            for k in range(2):
-                for part in range(2):
-                    at = 2 * field + k
-                    edge_send[side, part, at : at + 1] = stage[field, k, part, row : row + 1]
-
-    for copy in early[:2]:
+
+    def pack(n, row_of):
+        for side in range(2):
+            row = row_of[side]
+            for field in range(2):
+                for k in range(2):
+                    for part in range(2):
+                        at = 2 * field + k
+                        edge_send[side, n, part, at : at + 1] = stage[field, k, part, row : row + 1]
+
+    pack(0, (0, 2 * ROWS - 1))
+    for copy in nears:
         copy.start()
     angs = remote_copy(angb.at[my_slots], angb.at[my_slots], sib)
     fields = [
         remote_copy(ref.at[:, :, theirs], first.at[k, my_slots], sib)
         for k, ref in enumerate(fields_hbm)
     ]
-    sends += models + [angs] + fields + early
+    sends += models[2:] + [angs] + fields + slows + seconds
+    pack(1, (1, 2 * ROWS - 2))
+    for side, row in ((0, 0), (1, 2 * ROWS - 1)):
+        for k in range(2):
+            for part in range(2):
+                edge_a_send[side, part, k : k + 1] = stage[2, k, part, row : row + 1]
+    for copy in models[:2] + nears:
+        copy.wait_send()
+    for copy in seconds:
+        copy.start()
     for copy in [angs] + models:
         copy.wait_recv()
 
@@ -331,24 +368,81 @@
             device_id_type=MESH,
         )
 
-    def first_edges():
-        slow_row = slow_recv[slabs[0]]
-        rows4 = lax.broadcasted_iota(jnp.int32, (4, ni), 0)
+    rows8 = lax.broadcasted_iota(jnp.int32, (8, 128), 0)
+    edge_ang = jnp.where(
+        rows8 < 4,
+        jnp.where(rows8 % 2 == 0, angb[0], angb[1]),
+        jnp.where(rows8 % 2 == 0, angb[2], angb[3]),
+    )
+    edge_sign = wide(jnp.where(rows8 % 4 < 2, 1.0, -1.0))
+
+    def edge_rotated(n, cosine, sine):
         for core in range(2):
-            tile = jnp.where(
-                lax.broadcasted_iota(jnp.int32, (4, 128), 0) % 2 == 0,
-                angb[2 * core, 0:4],
-                angb[2 * core + 1, 0:4],
-            )
-            cosine, sine = cos_sin(wide(tile) * slow_row)
-            sine = jnp.where(rows4 < 2, sine, -sine)
-            p, q = edge_recv[core, 0], edge_recv[core, 1]
-            real, imag = p * cosine - q * sine, p * sine + q * cosine
+            for part in range(2):
+                edge_raw[n, part, 4 * core : 4 * core + 4] = edge_recv[core, n, part]
+        p, q = edge_raw[n, 0], edge_raw[n, 1]
+        return p * cosine - q * sine, p * sine + q * cosine
+
+    def put_edges(z, real, imag):
+        for core in range(2):
             for field in range(2):
                 for k in range(2):
-                    at = 2 * field + k
-                    halo_sr[0, c, 2 * core + k, 2 * field : 2 * field + 1] = real[at : at + 1]
-                    halo_sr[0, c, 2 * core + k, 2 * field + 1 : 2 * field + 2] = imag[at : at + 1]
+                    at = 4 * core + 2 * field + k
+                    for part, value in enumerate((real, imag)):
+                        j = 2 * field + part
+                        halo_sr[z, c, 2 * core + k, j : j + 1] = value[at : at + 1]
+
+    def first_edges():
+        cosine, sine = cos_sin(wide(edge_ang) * slow_recv[slabs[0], 0])
+        real, imag = edge_rotated(0, cosine, sine * edge_sign)
+        edge_near[0] = real
+        edge_near[1] = imag
+        put_edges(0, real, imag)
+
+    def beside(v):
+        before = pltpu.roll(v, 1, 1)
+        before = jnp.concatenate(
+            [jnp.where(lanes == 0, 0.0, before[:, :128]), before[:, 128:]], axis=1
+        )
+        after = pltpu.roll(v, ni - 1, 1)
+        after = jnp.concatenate(
+            [after[:, :-128], jnp.where(lanes == 127, 0.0, after[:, -128:])], axis=1
+        )
+        return before + after
+
+    def second_edges():
+        cosine, sine = cos_sin(wide(edge_ang) * slow_recv[slabs[0], 1])
+        far_r, far_i = edge_rotated(1, cosine, sine * edge_sign)
+        for core in range(2):
+            for field in range(2):
+                for k in range(2):
+                    at = 4 * core + 2 * field + k
+                    for part in range(2):
+                        j = 2 * field + part
+                        edge_raw[0, part, at : at + 1] = row_sr[0, c, 2 * core + k, j : j + 1]
+        vr, vi = edge_near[0], edge_near[1]
+        lap_r = (edge_raw[0, 0] + far_r) + beside(vr) - 4.0 * vr
+        lap_i = (edge_raw[0, 1] + far_i) + beside(vi) - 4.0 * vi
+        coupling = edge_sign * wide(DISPERSE * BASE_FREQ / edge_ang) * slow_recv[slabs[0], 2]
+        p = vr + DIFFUSE * lap_r - coupling * lap_i
+        q = vi + DIFFUSE * lap_i + coupling * lap_r
+        cosine, sine = cos_sin(wide(edge_ang) * slow_recv[slabs[1], 0])
+        sine = sine * edge_sign
+        put_edges(1, p * cosine - q * sine, p * sine + q * cosine)
+
+    def adjoint_edges():
+        cosine, sine = cos_sin(wide(edge_ang) * slow_recv[slabs[0], 0])
+        for core in range(2):
+            for part in range(2):
+                for twice in range(2):
+                    at = 4 * core + 2 * twice
+                    edge_raw[2, part, at : at + 2] = edge_a_recv[core, part]
+        p, q = edge_raw[2, 0], edge_raw[2, 1]
+        for part, value in enumerate((p * cosine + q * sine, q * cosine - p * sine)):
+            for core in range(2):
+                for k in range(2):
+                    at = 4 * core + k
+                    halo_a[0, c, 2 * core + k, part : part + 1] = value[at : at + 1]
 
     def first_sr(k, carry):
         rotate_sr(0, k, (first[0, k, 0], first[0, k, 1], first[1, k, 0], first[1, k, 1]))
@@ -362,7 +456,7 @@
     def pass_sr(z):
         def body(k, total):
             coupling = couple(z, k)
-            if z > 0:
+            if z > 1:
                 sr_outer(z, k).wait_recv()
             sr_inner(z, k).wait_recv()
             s_r, s_i = spread(vsr[k, 0], vsr[k, 1], halo_sr, z, k, 0, coupling)
@@ -371,7 +465,8 @@
                 sr[z, k, j] = value
             if z + 1 < STEPS:
                 rotate_sr(z + 1, k, (s_r, s_i, r_r, r_i))
-                sr_outer(z + 1, k).start()
+                if z > 0:
+                    sr_outer(z + 1, k).start()
                 sr_inner(z + 1, k).start()
             return total + (s_r * r_r + s_i * r_i)
 
@@ -413,7 +508,7 @@
         copy.wait_recv()
     lax.fori_loop(0, NF, first_sr, 0)
     for core in range(2):
-        edge_copy(0, core, sib).wait_recv()
+        edge_copy(0, 0, core, sib).wait_recv()
     for k in range(SLABS):
         slow_copy(0, k, sib).wait_recv()
     first_edges()
@@ -465,8 +560,15 @@
             own_fields[2].wait()
             fields[2].wait_recv()
             lax.fori_loop(0, NF, first_a, 0)
-            wait_a = send_rows(row_a, halo_a, 0)
+            wait_a = [remote_copy(row_a.at[0, o], halo_a.at[0, c], sib)]
             sends += wait_a
+        if z == 0:
+            for core in range(2):
+                edge_a_copy(0, core, sib).wait_recv()
+                edge_copy(0, 1, core, sib).wait_recv()
+            second_edges()
+        if z == 1:
+            adjoint_edges()
         if z + 2 < STEPS:
             trig(z + 2)
         if LAG == 0:
@@ -496,7 +598,7 @@
         copy.wait_send()
     for z in range(STEPS):
         for k in range(NF):
-            if z > 0:
+            if z > 1:
                 sr_outer(z, k).wait_send()
             sr_inner(z, k).wait_send()
 
@@ -549,16 +651,22 @@
             vmem(3, *half),
             pltpu.SMEM(args[6].shape, jnp.int32),
             pltpu.SMEM(args[7].shape, jnp.int32),
-            vmem(2, 2, 2, 2 * ROWS, ni),
-            vmem(2, 2, 4, ni),
-            vmem(2, 2, 4, ni),
-            vmem(2, 1, ni),
-            vmem(SLABS, 1, ni),
+            vmem(3, 2, 2, 2 * ROWS, ni),
+            vmem(2, 2, 2, 4, ni),
+            vmem(2, 2, 2, 4, ni),
+            vmem(2, 2, 2, ni),
+            vmem(2, 2, 2, ni),
+            vmem(3, 2, 8, ni),
+            vmem(2, 8, ni),
+            vmem(2, 3, 1, ni),
+            vmem(SLABS, 3, 1, ni),
             pltpu.SemaphoreType.DMA((24,)),
             pltpu.SemaphoreType.DMA((40,)),
             pltpu.SemaphoreType.DMA((40,)),
             pltpu.SemaphoreType.DMA((STEPS, NF, 2)),
             pltpu.SemaphoreType.DMA((STEPS, NF, 2)),
+            pltpu.SemaphoreType.DMA((2, 2)),
+            pltpu.SemaphoreType.DMA((2, 2)),
             pltpu.SemaphoreType.DMA((2,)),
             pltpu.SemaphoreType.DMA((2,)),
             pltpu.SemaphoreType.DMA((4,)),

time: 58.7 us -> 58.3 us (level)
  no operation moved by 1% of the time
where the time goes in v3:
time: 58.3 us; the launch traced here: 58.2 us
  Pallas kernels  57.5 us (99%)
  between operations  0.64 us (1%)
    pallas_call x1, Pallas kernels, step(): pl.pallas_call(functools.partial(kernel, bands), out_shape=(jax.ShapeDtyp...  56.4 us

profile of v3, /device:TPU:1, one launch (start us, length us, event | category | flops | bytes accessed | tf_op | source)
XLA Modules:
  0.0 58.2 jit_solution(1463759391788237423)
XLA Ops:
  0.6 56.4 %shard_map.103 = (f32[2,2,16,2048]{3,2,1,0:T(8,128)S(1)}, f32[4,16,2048]{2,1,0:T(8,128)S(1)}, f32[1,3,16,2048]{3,2,1,0:T(8,128)S(1)}) custom-call(f32[2,2,16,2048]{3,2,1,0:T(8,128)} %src_hbm.1, f32[2,2,16,2048]{3,2,1,0:T(8,128)} %rec_hbm.1, f32[2,2,16,2048]{3,2,1,0:T(8,128)} %adj_hbm.1, f32[1,16,2048]{2,1,0:T(8,128)} %slow_hbm.1, f32[1,16,2048]{2,1,0:T(8,128)} %eps_hbm.1, ...), custom_call_target="tpu_custom_call" | custom-call | tf_op jit(solution)/shard_map/pallas_call | solution.py:677
  57.0 1.1 %shard_map.104 = (f32[2,2,16,2048]{3,2,1,0:T(8,128)}, f32[4,16,2048]{2,1,0:T(8,128)}, f32[1,3,16,2048]{3,2,1,0:T(8,128)}) custom-call(f32[2,2,16,2048]{3,2,1,0:T(8,128)S(1)} %get-tuple-element.6.refs_0_, f32[4,16,2048]{2,1,0:T(8,128)S(1)} %get-tuple-element.7.refs_1_, f32[1,3,16,2048]{3,2,1,0:T(8,128)S(1)} %get-tuple-element.8.refs_2_), custom_call_target="tpu_custom_call" | custom-call | tf_op jit(solution)/shard_map/pallas_call | solution.py:691

commit v4 on v3

--- a/solution.py
+++ b/solution.py
@@ -106,6 +106,8 @@
     recv_sem,
     sr_send_sem,
     sr_recv_sem,
+    a_send_sem,
+    a_recv_sem,
     edge_send_sem,
     edge_recv_sem,
     edge_a_send_sem,
@@ -342,11 +344,25 @@
             va[k, j] = value
             put_rows(row_a, z, k, j, value)
 
-    def send_rows(rows, halos, z):
-        return [
-            remote_copy(rows.at[z, c], halos.at[z, o], neighbour),
-            remote_copy(rows.at[z, o], halos.at[z, c], sib),
-        ]
+    def a_outer(z, k):
+        return pltpu.make_async_remote_copy(
+            src_ref=row_a.at[z, c, k],
+            dst_ref=halo_a.at[z, o, k],
+            send_sem=a_send_sem.at[z, k, 0],
+            recv_sem=a_recv_sem.at[z, k, 0],
+            device_id=neighbour,
+            device_id_type=MESH,
+        )
+
+    def a_inner(z, k):
+        return pltpu.make_async_remote_copy(
+            src_ref=row_a.at[z, o, k],
+            dst_ref=halo_a.at[z, c, k],
+            send_sem=a_send_sem.at[z, k, 1],
+            recv_sem=a_recv_sem.at[z, k, 1],
+            device_id=sib,
+            device_id_type=MESH,
+        )
 
     def sr_outer(z, k):
         return pltpu.make_async_remote_copy(
@@ -451,6 +467,7 @@
 
     def first_a(k, carry):
         rotate_a(0, k, first[2, k, 0], first[2, k, 1])
+        a_inner(0, k).start()
         return carry
 
     def pass_sr(z):
@@ -474,6 +491,9 @@
 
     def pass_a(z):
         def body(k, carry):
+            if z > 0:
+                a_outer(z, k).wait_recv()
+            a_inner(z, k).wait_recv()
             a_r, a_i = spread(va[k, 0], va[k, 1], halo_a, z, k, 0, -couple(z, k))
             adj[k, 0] = a_r
             adj[k, 1] = a_i
@@ -491,6 +511,8 @@
             a_i = adj[k, 1] + half * s_i
             if z + 1 < STEPS:
                 rotate_a(z + 1, k, a_r, a_i)
+                a_outer(z + 1, k).start()
+                a_inner(z + 1, k).start()
             else:
                 adj[k, 0] = a_r
                 adj[k, 1] = a_i
@@ -529,17 +551,11 @@
     arrivals = []
     gradients = []
 
-    def finish(z, wait_a, image):
-        for copy in wait_a:
-            copy.wait_recv()
+    def finish(z, image):
         pass_a(z)
         image.wait_recv()
         img[z] = (ipart[z] + irecv[z]) * (1.0 / (2 * NF))
         force(z)
-        wait_a = []
-        if z + 1 < STEPS:
-            wait_a = send_rows(row_a, halo_a, z + 1)
-            sends.extend(wait_a)
         if z >= STEPS - 2:
             n = z - (STEPS - 2)
             for j in range(3):
@@ -550,8 +566,6 @@
             copies.append(local_copy(adj.at[my_slots], adj_out.at[:, :, mine]))
         copies.append(local_copy(img.at[z], img_out.at[z, mine]))
         arrivals.append(remote_copy(img.at[z], img_out.at[z, mine], sib))
-        return wait_a
-
     images = []
     for z in range(STEPS):
         pass_sr(z)
@@ -560,8 +574,6 @@
             own_fields[2].wait()
             fields[2].wait_recv()
             lax.fori_loop(0, NF, first_a, 0)
-            wait_a = [remote_copy(row_a.at[0, o], halo_a.at[0, c], sib)]
-            sends += wait_a
         if z == 0:
             for core in range(2):
                 edge_a_copy(0, core, sib).wait_recv()
@@ -572,11 +584,11 @@
         if z + 2 < STEPS:
             trig(z + 2)
         if LAG == 0:
-            wait_a = finish(z, wait_a, images[z])
+            finish(z, images[z])
         elif z > 0:
-            wait_a = finish(z - 1, wait_a, images[z - 1])
+            finish(z - 1, images[z - 1])
     if LAG:
-        wait_a = finish(STEPS - 1, wait_a, images[STEPS - 1])
+        finish(STEPS - 1, images[STEPS - 1])
     sends += images
     sends += gradients
 
@@ -601,6 +613,9 @@
             if z > 1:
                 sr_outer(z, k).wait_send()
             sr_inner(z, k).wait_send()
+            if z > 0:
+                a_outer(z, k).wait_send()
+            a_inner(z, k).wait_send()
 
 
 def hand_over(*refs):
@@ -665,6 +680,8 @@
             pltpu.SemaphoreType.DMA((40,)),
             pltpu.SemaphoreType.DMA((STEPS, NF, 2)),
             pltpu.SemaphoreType.DMA((STEPS, NF, 2)),
+            pltpu.SemaphoreType.DMA((STEPS, NF, 2)),
+            pltpu.SemaphoreType.DMA((STEPS, NF, 2)),
             pltpu.SemaphoreType.DMA((2, 2)),
             pltpu.SemaphoreType.DMA((2, 2)),
             pltpu.SemaphoreType.DMA((2,)),

time: 58.3 us -> 58.1 us (level)
  no operation moved by 1% of the time
where the time goes in v4:
time: 58.1 us; the launch traced here: 58 us
  Pallas kernels  57.3 us (99%)
  between operations  0.64 us (1%)
    pallas_call x1, Pallas kernels, step(): pl.pallas_call(functools.partial(kernel, bands), out_shape=(jax.ShapeDtyp...  56.2 us

profile of v4, /device:TPU:1, one launch (start us, length us, event | category | flops | bytes accessed | tf_op | source)
XLA Modules:
  0.0 58.0 jit_solution(14985352821784306059)
XLA Ops:
  0.6 56.2 %shard_map.103 = (f32[2,2,16,2048]{3,2,1,0:T(8,128)S(1)}, f32[4,16,2048]{2,1,0:T(8,128)S(1)}, f32[1,3,16,2048]{3,2,1,0:T(8,128)S(1)}) custom-call(f32[2,2,16,2048]{3,2,1,0:T(8,128)} %src_hbm.1, f32[2,2,16,2048]{3,2,1,0:T(8,128)} %rec_hbm.1, f32[2,2,16,2048]{3,2,1,0:T(8,128)} %adj_hbm.1, f32[1,16,2048]{2,1,0:T(8,128)} %slow_hbm.1, f32[1,16,2048]{2,1,0:T(8,128)} %eps_hbm.1, ...), custom_call_target="tpu_custom_call" | custom-call | tf_op jit(solution)/shard_map/pallas_call | solution.py:694
  56.8 1.1 %shard_map.104 = (f32[2,2,16,2048]{3,2,1,0:T(8,128)}, f32[4,16,2048]{2,1,0:T(8,128)}, f32[1,3,16,2048]{3,2,1,0:T(8,128)}) custom-call(f32[2,2,16,2048]{3,2,1,0:T(8,128)S(1)} %get-tuple-element.6.refs_0_, f32[4,16,2048]{2,1,0:T(8,128)S(1)} %get-tuple-element.7.refs_1_, f32[1,3,16,2048]{3,2,1,0:T(8,128)S(1)} %get-tuple-element.8.refs_2_), custom_call_target="tpu_custom_call" | custom-call | tf_op jit(solution)/shard_map/pallas_call | solution.py:708
